TPU v7x, 256 devices: a whole 4x4x8 slice. The times are simulated.
256 devices in a mesh: group: 64 (over y_hi, z, x), tensor: 4 (over y_lo, core).
Axes of the slice: x: 4, y: 4 (y_hi: 2, y_lo: 2; y = y_hi * 2 + y_lo), z: 8, core: 2. Of those that a mesh axis runs over, the one named last changes fastest.
Arguments:
- hidden: bfloat16 [2, 1024, 4096], P(None, 'group'), may hold values from -6 to 6
- queries: bfloat16 [2, 1024, 32, 128], P(None, 'group', 'tensor'), may hold values from -4.5 to 4.5
- kv_cache: bfloat16 [2, 1024, 4, 256, 128], P(None, 'group', 'tensor'), may hold values from -4.5 to 4.5
- lengths: int32 [1024], P('group'), may hold values from 2 to 256, as said below
- frozen_key_value: bfloat16 [4096, 2, 512], P(None, None, 'tensor'), may hold values from -0.09375 to 0.09375
- frozen_output_weight: bfloat16 [4096, 4096], P('tensor'), may hold values from -0.09375 to 0.09375
- down_kv: bfloat16 [4096, 2, 32], P('group'), may hold values from -0.09375 to 0.09375
- up_kv: bfloat16 [2, 32, 4, 128], P(None, None, 'tensor', 'group'), may hold values from -1 to 1
- down_o: bfloat16 [32, 128, 32], P('tensor', 'group'), may hold values from -0.09375 to 0.09375
- up_o: bfloat16 [32, 4096], P(None, 'group'), may hold values from -1 to 1
Outputs:
- attended: bfloat16 [2, 1024, 4096], P(None, 'group')
- new_kv: bfloat16 [2, 2, 1024, 4, 128], P(None, None, 'group', 'tensor')
Inputs may be any that keep to these rules, and one draw needn't show every extreme that they name: `lengths`: at least one row has exactly 256.
All inputs are finite; a program needn't handle non-finite values.
Results may differ from a plain program's by a relative error of at most 0.0083.
Values may be sent and summed in bfloat16 or wider, within the bound.
A program may use at most 64 MiB of HBM per device.

v0:
```python
import math

import jax
import jax.numpy as jnp
from jax import lax
from jax.experimental import pallas as pl
from jax.experimental.pallas import tpu as pltpu
from jax.sharding import PartitionSpec as P

BF = jnp.bfloat16
F32 = jnp.float32
MESH = pl.DeviceIdType.MESH

ADAPTER_SCALE = 2.0
ROPE_BASE = 500000.0
SCALE = 1.0 / math.sqrt(128.0)
MASKED = -1e30
WIDTH = 512

NT = (((1,), (1,)), ((), ()))


def dot(a, b):
    return jnp.dot(a, b, preferred_element_type=F32)


def dot_nt(a, b):
    return lax.dot_general(a, b, NT, preferred_element_type=F32)


def place(rows, columns, offset):
    i = lax.broadcasted_iota(jnp.int32, (rows, columns), 0)
    j = lax.broadcasted_iota(jnp.int32, (rows, columns), 1)
    return jnp.where(j == i + offset, 1.0, 0.0).astype(BF)


def kernel(
    hid_hbm, q_hbm, kv_hbm, len_hbm, fkv_hbm, w_hbm, dkv_hbm, ukv_hbm, do_hbm, uo_hbm,
    att_hbm, nkv_hbm,
    hid, q_v, kv, fkv, w, dk_v, uk_v, do_v, uo_v,
    hx, qs, r1, gb, gt, uu, uo, hd, pu, pm, dm, s16, s4,
    zs, zr, zos, zor, acc, mm, ll, ctxs, ctx, u,
    ps, pr, ys, yr, fs, nk, nv, nst, base, len_ref,
    lsem, one, prs, yrs,
):
    a1s, a1r, a2s, a2r, b1s, b1r, b2s, b2r, ts, tr, os, orr, pss, yss, fss, frs, outs, outk, c2s, c2r, d2s, d2r = (one.at[i] for i in range(22))
    g = lax.axis_index("group")
    t = lax.axis_index("tensor")
    yh = lax.div(g, 32)
    z = lax.rem(lax.div(g, 4), 8)
    x = lax.rem(g, 4)
    yl = lax.div(t, 2)
    c = lax.rem(t, 2)

    def group_of(yh_, z_, x_):
        return yh_ * 32 + z_ * 4 + x_

    def tensor_of(k):
        yl_ = yl if k < 2 else 1 - yl
        c_ = c if k % 2 == 0 else 1 - c
        return yl_ * 2 + c_

    def remote(src, dst, ss, rs, group, tensor):
        return pltpu.make_async_remote_copy(
            src_ref=src, dst_ref=dst, send_sem=ss, recv_sem=rs,
            device_id={"group": group, "tensor": tensor}, device_id_type=MESH,
        )

    barrier = pltpu.get_barrier_semaphore()

    def xy_peer(k):
        return (yh if k < 4 else 1 - yh), lax.rem(x + k % 4, 4)

    def arrived(ref, sem):
        remote(ref, ref, ts, sem, g, t).wait_recv()

    def left(ref, sem):
        remote(ref, ref, sem, tr, g, t).wait_send()

    def load(src, dst, i):
        copy = pltpu.make_async_copy(src, dst, lsem.at[i])
        copy.start()
        return copy

    l_dk = load(dkv_hbm.at[pl.ds(pl.multiple_of(c * 32, 32), 32), :], dk_v, 0)
    l_uk = load(ukv_hbm, uk_v, 1)
    l_do = load(do_hbm, do_v, 2)
    l_uo = load(uo_hbm, uo_v, 3)

    def greet(group, tensor):
        pl.semaphore_signal(barrier, inc=1, device_id={"group": group, "tensor": tensor}, device_id_type=MESH)

    for hop, k in (
        ("xy", 6), ("z", 4), ("z", 3), ("z", 5), ("xy", 5), ("xy", 7), ("xy", 2), ("z", 2), ("z", 6),
        ("xy", 4), ("xy", 1), ("xy", 3), ("z", 1), ("z", 7), ("t", 2), ("t", 3), ("t", 1),
    ):
        if hop == "z":
            greet(group_of(yh, lax.rem(z + k, 8), x), t)
        elif hop == "xy":
            greet(group_of(xy_peer(k)[0], z, xy_peer(k)[1]), t)
        else:
            greet(g, tensor_of(k))

    l_hid = load(hid_hbm, hid, 4)
    l_q = load(q_hbm, q_v, 5)
    l_fkv = load(fkv_hbm, fkv, 6)
    l_kv = load(kv_hbm, kv, 7)
    l_len = load(len_hbm, len_ref, 9)
    l_w = load(w_hbm, w, 8)

    m = lax.rem(z, 4)
    q = lax.rem(m + jnp.where(z < 4, 1, 2), 4)
    l_dk.wait()
    l_uk.wait()
    l_do.wait()
    for h in range(8):
        s16[2 * h : 2 * h + 2, :] = do_v[h].astype(F32)
    for k in range(2):
        for i in range(4):
            s4[4 * i + 2 * k : 4 * i + 2 * k + 2, :] = uk_v[k].astype(F32)
    row16 = lax.broadcasted_iota(jnp.int32, (16, 32), 0)
    up_rows = jnp.where(jnp.logical_and(row16 >= 4 * m, row16 < 4 * m + 4), s4[...], 0.0)
    half = dk_v[...]
    r1[z, 0] = (dot(half[0:16], place(64, 128, 0)) + dot(half[16:32], place(64, 128, 64))).astype(BF)
    r1[z, 1] = (
        dot(s16[...].astype(BF), place(32, 128, 32 * m)) + dot(up_rows.astype(BF), place(32, 128, 32 * q))
    ).astype(BF)
    l_uo.wait()

    @pl.when(yh == c)
    def _():
        up = uo_v[...]
        gb[z, x] = (dot(up[0:16], place(64, 128, 0)) + dot(up[16:32], place(64, 128, 64))).astype(BF)

    lane = lax.broadcasted_iota(jnp.int32, (32, 128), 1)
    pl.semaphore_wait(barrier, 17)

    for k in (4, 3, 5, 2, 6, 1, 7):
        remote(r1.at[z], r1.at[z], a1s, a1r, group_of(yh, lax.rem(z + k, 8), x), t).start()

    feature = lax.broadcasted_iota(jnp.int32, (128, 256), 0)
    source = lax.broadcasted_iota(jnp.int32, (128, 256), 1)

    def digit(value, shift, mask):
        return jnp.bitwise_and(lax.shift_right_logical(value, shift), mask)

    tile = digit(feature, 6, 1) * 4 + digit(feature, 1, 3)
    from_up = (tile * 16 + 4 * digit(feature, 3, 3) + digit(feature, 0, 1))[:, :128]
    from_down = tile * 32 + 16 * digit(feature, 5, 1) + digit(feature, 0, 1)
    for i in range(2):
        pu[i] = jnp.where(source[:, :128] == from_up + 2 * i, 1.0, 0.0).astype(BF)
    for h in range(8):
        pm[h] = jnp.where(source == from_down + 2 * h, 1.0, 0.0).astype(BF)
    square = lax.broadcasted_iota(jnp.int32, (128, 128), 0)
    lane_group = digit(lax.broadcasted_iota(jnp.int32, (128, 128), 1), 5, 3)
    up_lanes = lane_group == digit(digit(square, 3, 3) + 1 + digit(square, 5, 1), 0, 3)
    down_lanes = lane_group == digit(square, 3, 3)

    l_len.wait()
    sub = lax.broadcasted_iota(jnp.int32, (32, 128), 0)
    later = jnp.where(sub >= 16, 1, 0)
    in_step = sub - 16 * later
    position = later
    for r in range(16):
        position = position + jnp.where(in_step == r, len_ref[r], 0)
    counter = jnp.where(lane < 64, lane, lane - 64).astype(F32)
    angle = position.astype(F32) * jnp.exp(counter * (-2.0 * math.log(ROPE_BASE) / 128))
    cosine = jnp.cos(angle)
    sine = jnp.sin(angle)
    sine = jnp.where(lane < 64, -sine, sine)

    l_hid.wait()
    row = lax.broadcasted_iota(jnp.int32, (128, 512), 0)
    col = lax.broadcasted_iota(jnp.int32, (128, 512), 1)
    spread = jnp.where(jnp.where(col < 256, col, col - 257) == 2 * row, 1.0, 0.0).astype(BF)

    def spread_chunk(a, _):
        part = dot(hid[:, pl.ds(pl.multiple_of(a * 128, 128), 128)], spread).astype(BF)
        at = pl.ds(pl.multiple_of(a * 256, 256), 256)
        hx[0:32, at] = part[:, :256]
        hx[32:64, at] = part[:, 256:]
        return 0

    lax.fori_loop(0, 32, spread_chunk, 0, unroll=8)

    for a in range(32):
        pair = hid[:, a * 128 : a * 128 + 128].astype(F32)
        turned = pltpu.roll(pair, 64, 1)
        at = ((a // 16) * 4 + 2 * (a % 2)) * 1024 + (a // 2 % 8) * 128
        hd[0:32, at : at + 128] = jnp.where(lane < 64, pair, 0.0).astype(BF)
        hd[32:64, at : at + 128] = jnp.where(lane < 64, 0.0, turned).astype(BF)
        at = at + 1024
        hd[0:32, at : at + 128] = jnp.where(lane < 64, turned, 0.0).astype(BF)
        hd[32:64, at : at + 128] = jnp.where(lane < 64, 0.0, pair).astype(BF)

    l_fkv.wait()

    def project(a, total):
        at = pl.ds(pl.multiple_of(a * 1024, 1024), 1024)
        return total + dot(hx[:, at], fkv[at, :])

    base[...] = lax.fori_loop(0, 8, project, jnp.zeros((64, 128), F32), unroll=4)

    lane16 = lax.broadcasted_iota(jnp.int32, (16, 128), 1)
    block = yh * 4 + x
    arrived(r1.at[0:7], a1r)
    for z_ in range(8):
        gt[:, pl.ds(pl.multiple_of(block * 1024 + z_ * 128, 128), 128)] = r1[z_, 0]
    own_lanes = gt.at[:, pl.ds(pl.multiple_of(block * 1024, 1024), 1024)]
    for k in (6, 2, 5, 7, 4, 1, 3):
        yh_, x_ = xy_peer(k)
        remote(own_lanes, own_lanes, a2s, a2r, group_of(yh_, z, x_), t).start()
    others = [r1[z_, 1].astype(F32) for z_ in range(8)]

    def lanes_of(z_, i):
        return jnp.where(jnp.logical_and(lane16 >= 32 * i, lane16 < 32 * i + 32), others[z_], 0.0)

    uu[block] = sum(lanes_of(z_, (z_ % 4 + 1 + z_ // 4) % 4) for z_ in range(8)).astype(BF)
    uo[block, 0:16] = sum(lanes_of(z_, z_) for z_ in range(4)).astype(BF)
    uo[block, 16:32] = sum(lanes_of(z_, z_ - 4) for z_ in range(4, 8)).astype(BF)
    for ref, sent, came in ((uu, c2s, c2r), (uo, d2s, d2r)):
        for k in (6, 2, 5, 7, 4, 1, 3):
            yh_, x_ = xy_peer(k)
            remote(ref.at[block], ref.at[block], sent, came, group_of(yh_, z, x_), t).start()

    @pl.when(yh == c)
    def _():
        for k in (4, 3, 5, 2, 6, 1, 7):
            remote(gb.at[z, x], gb.at[z, x], b1s, b1r, group_of(yh, lax.rem(z + k, 8), x), t).start()

    l_q.wait()
    for s in range(2):
        qs[:, s * 8 : s * 8 + 8, :] = q_v[s].astype(F32)
    l_kv.wait()
    slots = lax.broadcasted_iota(jnp.int32, (16, 256), 1)

    def cached(r, _):
        scores = dot_nt(qs[r].astype(BF), kv[r]) * SCALE
        scores = jnp.where(slots < len_ref[r], scores, MASKED)
        top = jnp.max(scores, axis=1, keepdims=True)
        expo = jnp.exp(scores - top)
        acc[r] = dot(expo.astype(BF), kv[16 + r])
        mm[r] = jnp.broadcast_to(top, (16, 128))
        ll[r] = jnp.broadcast_to(jnp.sum(expo, axis=1, keepdims=True), (16, 128))
        return 0

    lax.fori_loop(0, 16, cached, 0, unroll=8)
    u[...] = jnp.zeros_like(u)

    arrived(gt.at[:, 0:7168], a2r)
    zs[...] = dot_nt(hd[...], gt[...]).astype(BF)
    remote(zs, zr, ts, tr, g, tensor_of(1)).start()

    @pl.when(yh == c)
    def _():
        arrived(gb.at[0:7, x], b1r)
        for k in (6, 2, 5, 7, 4, 1, 3):
            yh_, x_ = xy_peer(k)
            remote(gb.at[:, x], gb.at[:, x], b2s, b2r, group_of(yh_, z, x_), t).start()

    arrived(uu.at[0:7], c2r)
    gathered = uu[...].reshape(128, 128)
    ups = []
    for i in range(2):
        up = jnp.where(up_lanes, dot(pu[i], gathered), 0.0)
        up = up + pltpu.roll(up, 64, 1)
        up = up + pltpu.roll(up, 32, 1)
        ups.append((up[:, 0:16].astype(BF), pltpu.roll(up, 112, 1)[:, 0:16].astype(BF)))
    arrived(uo.at[0:7], d2r)
    gathered = uo[...].reshape(256, 128)
    for h in range(8):
        dm[h * 128 : h * 128 + 128, :] = jnp.where(down_lanes, dot(pm[h], gathered), 0.0).astype(BF)
    arrived(zr, tr)
    z_key = jnp.where(c == 0, zs[...], zr[...])
    z_value = jnp.where(c == 0, zr[...], zs[...])
    key = base[0:32, :] + ADAPTER_SCALE * (dot_nt(z_key[0:32], ups[0][0]) + dot_nt(z_key[32:64], ups[0][1]))
    value = base[32:64, :] + ADAPTER_SCALE * (dot_nt(z_value[0:32], ups[1][0]) + dot_nt(z_value[32:64], ups[1][1]))
    key = (key * cosine + pltpu.roll(key, 64, 1) * sine).astype(BF)
    value = value.astype(BF)
    nk[...] = key.astype(F32)
    nv[...] = value.astype(F32)
    first_step = lax.broadcasted_iota(jnp.int32, (16, 128), 0) < 8
    for r in range(16):
        query = qs[r]
        s0 = jnp.sum(query * nk[r : r + 1, :], axis=1, keepdims=True) * SCALE
        s1 = jnp.sum(query * nk[16 + r : 17 + r, :], axis=1, keepdims=True) * SCALE
        s0 = jnp.broadcast_to(s0, (16, 128))
        s1 = jnp.where(first_step, MASKED, jnp.broadcast_to(s1, (16, 128)))
        top = jnp.maximum(mm[r], jnp.maximum(s0, s1))
        alpha = jnp.exp(mm[r] - top)
        p0 = jnp.exp(s0 - top)
        p1 = jnp.exp(s1 - top)
        total = alpha * ll[r] + p0 + p1
        ctxs[r * 16 : r * 16 + 16, :] = (alpha * acc[r] + p0 * nv[r : r + 1, :] + p1 * nv[16 + r : 17 + r, :]) / total
    for s in range(2):
        for h in range(8):
            ctx[s * 16 : s * 16 + 16, h * 128 : h * 128 + 128] = ctxs[pl.ds(s * 8 + h, 16, stride=16), :].astype(BF)

    context = ctx[...]

    l_w.wait()
    core_peer = tensor_of(1)
    chip_peer = tensor_of(2)

    def part(ref, j):
        return ref.at[:, pl.ds(pl.multiple_of(j * WIDTH, WIDTH), WIDTH)]

    def columns(half, j):
        return pl.ds(pl.multiple_of(half * 2048 + j * WIDTH, WIDTH), WIDTH)

    def give_copy(j):
        return remote(part(ps, j), part(pr, j), pss, prs.at[j], g, core_peer)

    def chip_copy(j):
        return remote(part(ys, j), part(yr, j), yss, yrs.at[j], g, chip_peer)

    def final_copy(j):
        return remote(part(fs, j), att_hbm.at[:, columns(c, j)], fss, frs, g, core_peer)

    def local_copy(j):
        return pltpu.make_async_copy(part(fs, j), att_hbm.at[:, columns(c, j)], outs)

    def give(j, _):
        part(ps, j)[...] = dot(context, w[:, columns(1 - c, j)]).astype(BF)
        give_copy(j).start()
        return 0

    def keep(j, _):
        total = dot(context, w[:, columns(c, j)])
        give_copy(j).wait_recv()
        part(ys, j)[...] = (total + part(pr, j)[...].astype(F32)).astype(BF)
        chip_copy(j).start()
        return 0

    def finish(j, _):
        term = dot(low_sum, part(u, j)[...])
        chip_copy(j).wait_recv()
        part(fs, j)[...] = ((part(ys, j)[...].astype(F32) + part(yr, j)[...].astype(F32)) + term).astype(BF)
        final_copy(j).start()
        local_copy(j).start()
        return 0

    lax.fori_loop(0, 2048 // WIDTH, give, 0)

    for s in range(2):
        nst[s, 0] = key[s * 16 : s * 16 + 16]
        nst[s, 1] = value[s * 16 : s * 16 + 16]
    l_nkv = pltpu.make_async_copy(nst, nkv_hbm, outk)
    l_nkv.start()

    low = dot(context, dm[...])
    low = low + pltpu.roll(low, 64, 1)
    low = low + pltpu.roll(low, 32, 1)
    lane8 = lax.broadcasted_iota(jnp.int32, (8, 128), 1)
    zos[...] = jnp.where(
        lane8 < 64,
        jnp.where(lane8 < 32, low[0:8], low[8:16]),
        jnp.where(lane8 < 96, low[16:24], low[24:32]),
    )
    for k in (2, 3, 1):
        remote(zos, zor.at[k], os, orr, g, tensor_of(k)).start()

    lax.fori_loop(0, 2048 // WIDTH, keep, 0)

    @pl.when(yh == c)
    def _():
        arrived(gb.at[:, 0:3], b2r)

    @pl.when(yh != c)
    def _():
        arrived(gb, b2r)

    for a in range(16):
        even = gb[a // 2, 2 * (a % 2)].astype(F32)
        odd = gb[a // 2, 2 * (a % 2) + 1].astype(F32)
        u[64:80, a * 128 : a * 128 + 128] = jnp.where(lane16 < 64, even, pltpu.roll(odd, 64, 1)).astype(BF)
        u[80:96, a * 128 : a * 128 + 128] = jnp.where(lane16 < 64, pltpu.roll(even, 64, 1), odd).astype(BF)
    arrived(zor.at[1:4], orr)
    low = (zos[...] + zor[1]) + (zor[2] + zor[3])
    low_sum = jnp.concatenate([pltpu.roll(low, 64, 1), pltpu.roll(low, 32, 1), low, pltpu.roll(low, 96, 1)], axis=0)
    low_sum = jnp.where(jnp.logical_and(lane >= 64, lane < 96), ADAPTER_SCALE * low_sum, 0.0).astype(BF)
    lax.fori_loop(0, 2048 // WIDTH, finish, 0)

    left(r1.at[0:7], a1s)
    left(gt.at[:, 0:7168], a2s)
    left(uu.at[0:7], c2s)
    left(uo.at[0:7], d2s)
    left(zs, ts)
    left(zor.at[1:4], os)
    left(ps, pss)
    left(ys, yss)
    left(fs, fss)

    @pl.when(yh == c)
    def _():
        left(gb.at[0:7, x], b1s)
        left(gt.at[:, 0:7168], b2s)

    l_nkv.wait()
    pltpu.make_async_copy(fs, fs, outs).wait()
    arrived(fs, frs)


def store(att_in, nkv_in, att_out, nkv_out, sems):
    first = pltpu.make_async_copy(att_in, att_out, sems.at[0])
    second = pltpu.make_async_copy(nkv_in, nkv_out, sems.at[1])
    first.start()
    second.start()
    first.wait()
    second.wait()


def local(hidden, queries, kv_cache, lengths, frozen_key_value, frozen_output_weight, down_kv, up_kv, down_o, up_o):
    hbm = pl.BlockSpec(memory_space=pltpu.HBM)
    dma = pltpu.SemaphoreType.DMA
    args = (
        hidden.reshape(32, 4096),
        queries,
        kv_cache.reshape(32, 256, 128),
        lengths,
        frozen_key_value.reshape(8192, 128),
        frozen_output_weight,
        down_kv.transpose(1, 2, 0).reshape(64, 64),
        up_kv.transpose(0, 2, 3, 1).reshape(2, 2, 32),
        down_o,
        up_o,
    )
    args = tuple(pltpu.with_memory_space_constraint(a, pltpu.HBM) for a in args)
    v = pltpu.VMEM
    attended, new_kv = pl.pallas_call(
        kernel,
        out_shape=(pltpu.VMEM((32, 4096), BF), pltpu.VMEM((2, 2, 16, 128), BF)),
        in_specs=[hbm] * 10,
        out_specs=(hbm, hbm),
        scratch_shapes=[
            v((32, 4096), BF), v((2, 16, 8, 128), BF), v((32, 256, 128), BF), v((8192, 128), BF), v((1024, 4096), BF),
            v((32, 64), BF), v((2, 2, 32), BF), v((8, 2, 32), BF), v((32, 64), BF),
            v((64, 8192), BF), v((16, 16, 128), F32), v((8, 2, 16, 128), BF), v((8, 4, 16, 128), BF),
            v((16, 8192), BF), v((8, 16, 128), BF), v((8, 32, 128), BF), v((64, 8192), BF), v((2, 128, 128), BF), v((8, 128, 256), BF), v((1024, 128), BF),
            v((16, 32), F32), v((16, 32), F32),
            v((64, 16), BF), v((64, 16), BF), v((8, 128), F32), v((4, 8, 128), F32),
            v((16, 16, 128), F32), v((16, 16, 128), F32), v((16, 16, 128), F32), v((256, 128), F32),
            v((32, 1024), BF), v((128, 2048), BF),
            v((32, 2048), BF), v((32, 2048), BF), v((32, 2048), BF), v((32, 2048), BF), v((32, 2048), BF),
            v((32, 128), F32), v((32, 128), F32), v((2, 2, 16, 128), BF), v((64, 128), F32), pltpu.SMEM((16,), jnp.int32),
            dma((10,)), dma((22,)), dma((2048 // WIDTH,)), dma((2048 // WIDTH,)),
        ],
        compiler_params=pltpu.CompilerParams(
            collective_id=0, has_side_effects=True, vmem_limit_bytes=40 * 1024 * 1024
        ),
    )(*args)
    attended, new_kv = pl.pallas_call(
        store,
        out_shape=(pltpu.HBM((32, 4096), BF), pltpu.HBM((2, 2, 16, 128), BF)),
        in_specs=[hbm, hbm],
        out_specs=(hbm, hbm),
        scratch_shapes=[dma((2,))],
    )(pltpu.with_memory_space_constraint(attended, pltpu.VMEM), pltpu.with_memory_space_constraint(new_kv, pltpu.VMEM))
    return attended.reshape(2, 16, 4096), new_kv.reshape(2, 2, 16, 1, 128)


def solution(mesh):
    placed = (
        P(None, "group", None),
        P(None, "group", "tensor", None),
        P(None, "group", "tensor", None, None),
        P("group"),
        P(None, None, "tensor"),
        P("tensor", None),
        P("group", None, None),
        P(None, None, "tensor", "group"),
        P("tensor", "group", None),
        P(None, "group"),
    )
    return jax.shard_map(
        local,
        mesh=mesh,
        in_specs=placed,
        out_specs=(P(None, "group", None), P(None, None, "group", "tensor", None)),
        check_vma=False,
    )
```

profile of v0, /device:TPU:1, one launch (start us, length us, event | category | flops | bytes accessed | tf_op | source)
XLA Modules:
  0.0 31.8 jit_solution(7033848353518683591)
XLA Ops:
  0.6 30.5 %shard_map.113 = (bf16[32,4096]{1,0:T(8,128)(2,1)S(1)}, bf16[2,2,16,128]{3,2,1,0:T(8,128)(2,1)S(1)}) custom-call(bf16[32,4096]{1,0:T(8,128)(2,1)} %bitcast.15, bf16[2,16,8,128]{3,2,1,0:T(8,128)(2,1)} %q_hbm.1, bf16[32,256,128]{2,1,0:T(8,128)(2,1)} %bitcast.13, s32[16]{0:T(128)} %len_hbm.1, bf16[8192,128]{1,0:T(8,128)(2,1)} %bitcast.14, ...), custom_call_target="tpu_custom_call" | custom-call | tf_op jit(solution)/shard_map/pallas_call | solution.py:430
  31.1 0.7 %shard_map.114 = (bf16[32,4096]{1,0:T(8,128)(2,1)}, bf16[2,2,16,128]{3,2,1,0:T(8,128)(2,1)}) custom-call(bf16[32,4096]{1,0:T(8,128)(2,1)S(1)} %get-tuple-element.6.att_in, bf16[2,2,16,128]{3,2,1,0:T(8,128)(2,1)S(1)} %get-tuple-element.7.nkv_in), custom_call_target="tpu_custom_call" | custom-call | tf_op jit(solution)/shard_map/pallas_call | solution.py:452
where the time goes:
time: 32 us; the launch traced here: 31.8 us
  Pallas kernels  31.2 us (98%)
  between operations  0.64 us (2%)
    pallas_call x1, Pallas kernels, local(): pl.pallas_call(kernel, out_shape=(pltpu.VMEM((32, 4096), BF), pltpu.VMEM(...  30.5 us
    pallas_call x1, Pallas kernels, local(): pl.pallas_call(store, out_shape=(pltpu.HBM((32, 4096), BF), pltpu.HBM((2,...  0.72 us

commit v1 on v0

--- a/solution.py
+++ b/solution.py
@@ -38,12 +38,12 @@
     hid_hbm, q_hbm, kv_hbm, len_hbm, fkv_hbm, w_hbm, dkv_hbm, ukv_hbm, do_hbm, uo_hbm,
     att_hbm, nkv_hbm,
     hid, q_v, kv, fkv, w, dk_v, uk_v, do_v, uo_v,
-    hx, qs, r1, gb, gt, uu, uo, hd, pu, pm, dm, s16, s4,
+    hx, qs, r1, gb, gt, uo, hd, pu, pm, dm, s16, s4,
     zs, zr, zos, zor, acc, mm, ll, ctxs, ctx, u,
-    ps, pr, ys, yr, fs, nk, nv, nst, base, len_ref,
-    lsem, one, prs, yrs,
+    ps, pr, ys, yr, fs, nk, nv, nst, base, sc, pe, len_ref,
+    lsem, one, prs, yrs, came,
 ):
-    a1s, a1r, a2s, a2r, b1s, b1r, b2s, b2r, ts, tr, os, orr, pss, yss, fss, frs, outs, outk, c2s, c2r, d2s, d2r = (one.at[i] for i in range(22))
+    a1s, a1r, a2s, a2r, b1s, b1r, b2s, b2r, ts, tr, os, orr, pss, yss, fss, frs, outs, outk, c2s, c2r = (one.at[i] for i in range(20))
     g = lax.axis_index("group")
     t = lax.axis_index("tensor")
     yh = lax.div(g, 32)
@@ -201,6 +201,25 @@
 
     base[...] = lax.fori_loop(0, 8, project, jnp.zeros((64, 128), F32), unroll=4)
 
+    l_q.wait()
+    for s in range(2):
+        qs[:, s * 8 : s * 8 + 8, :] = q_v[s].astype(F32)
+    l_kv.wait()
+    for r in range(16):
+        sc[r] = dot_nt(qs[r].astype(BF), kv[r])
+
+    slots = lax.broadcasted_iota(jnp.int32, (16, 256), 1)
+    for r in range(16):
+        scores = jnp.where(slots < len_ref[r], sc[r] * SCALE, MASKED)
+        top = jnp.max(scores, axis=1, keepdims=True)
+        expo = jnp.exp(scores - top)
+        pe[r] = expo.astype(BF)
+        mm[r] = jnp.broadcast_to(top, (16, 128))
+        ll[r] = jnp.broadcast_to(jnp.sum(expo, axis=1, keepdims=True), (16, 128))
+    for r in range(16):
+        acc[r] = dot(pe[r], kv[16 + r])
+    u[...] = jnp.zeros_like(u)
+
     lane16 = lax.broadcasted_iota(jnp.int32, (16, 128), 1)
     block = yh * 4 + x
     arrived(r1.at[0:7], a1r)
@@ -209,46 +228,35 @@
     own_lanes = gt.at[:, pl.ds(pl.multiple_of(block * 1024, 1024), 1024)]
     for k in (6, 2, 5, 7, 4, 1, 3):
         yh_, x_ = xy_peer(k)
-        remote(own_lanes, own_lanes, a2s, a2r, group_of(yh_, z, x_), t).start()
+        remote(own_lanes, own_lanes, a2s, came.at[k], group_of(yh_, z, x_), t).start()
     others = [r1[z_, 1].astype(F32) for z_ in range(8)]
 
     def lanes_of(z_, i):
         return jnp.where(jnp.logical_and(lane16 >= 32 * i, lane16 < 32 * i + 32), others[z_], 0.0)
 
-    uu[block] = sum(lanes_of(z_, (z_ % 4 + 1 + z_ // 4) % 4) for z_ in range(8)).astype(BF)
-    uo[block, 0:16] = sum(lanes_of(z_, z_) for z_ in range(4)).astype(BF)
-    uo[block, 16:32] = sum(lanes_of(z_, z_ - 4) for z_ in range(4, 8)).astype(BF)
-    for ref, sent, came in ((uu, c2s, c2r), (uo, d2s, d2r)):
-        for k in (6, 2, 5, 7, 4, 1, 3):
-            yh_, x_ = xy_peer(k)
-            remote(ref.at[block], ref.at[block], sent, came, group_of(yh_, z, x_), t).start()
+    uo[block, 0:16] = sum(lanes_of(z_, (z_ % 4 + 1 + z_ // 4) % 4) for z_ in range(8)).astype(BF)
+    uo[block, 16:32] = sum(lanes_of(z_, z_) for z_ in range(4)).astype(BF)
+    uo[block, 32:48] = sum(lanes_of(z_, z_ - 4) for z_ in range(4, 8)).astype(BF)
+    for k in (6, 2, 5, 7, 4, 1, 3):
+        yh_, x_ = xy_peer(k)
+        remote(uo.at[block], uo.at[block], c2s, c2r, group_of(yh_, z, x_), t).start()
 
     @pl.when(yh == c)
     def _():
         for k in (4, 3, 5, 2, 6, 1, 7):
             remote(gb.at[z, x], gb.at[z, x], b1s, b1r, group_of(yh, lax.rem(z + k, 8), x), t).start()
 
-    l_q.wait()
-    for s in range(2):
-        qs[:, s * 8 : s * 8 + 8, :] = q_v[s].astype(F32)
-    l_kv.wait()
-    slots = lax.broadcasted_iota(jnp.int32, (16, 256), 1)
-
-    def cached(r, _):
-        scores = dot_nt(qs[r].astype(BF), kv[r]) * SCALE
-        scores = jnp.where(slots < len_ref[r], scores, MASKED)
-        top = jnp.max(scores, axis=1, keepdims=True)
-        expo = jnp.exp(scores - top)
-        acc[r] = dot(expo.astype(BF), kv[16 + r])
-        mm[r] = jnp.broadcast_to(top, (16, 128))
-        ll[r] = jnp.broadcast_to(jnp.sum(expo, axis=1, keepdims=True), (16, 128))
-        return 0
-
-    lax.fori_loop(0, 16, cached, 0, unroll=8)
-    u[...] = jnp.zeros_like(u)
-
-    arrived(gt.at[:, 0:7168], a2r)
-    zs[...] = dot_nt(hd[...], gt[...]).astype(BF)
+
+    def down_part(from_block):
+        at = pl.ds(pl.multiple_of(from_block * 1024, 1024), 1024)
+        return dot_nt(hd[:, at], gt[:, at])
+
+    low = down_part(block)
+    for k in (1, 3, 4, 2, 7, 5, 6):
+        from_block = (yh if k < 4 else 1 - yh) * 4 + lax.rem(x + 4 - k % 4, 4)
+        arrived(gt.at[:, pl.ds(pl.multiple_of(from_block * 1024, 1024), 1024)], came.at[k])
+        low = low + down_part(from_block)
+    zs[...] = low.astype(BF)
     remote(zs, zr, ts, tr, g, tensor_of(1)).start()
 
     @pl.when(yh == c)
@@ -258,16 +266,15 @@
             yh_, x_ = xy_peer(k)
             remote(gb.at[:, x], gb.at[:, x], b2s, b2r, group_of(yh_, z, x_), t).start()
 
-    arrived(uu.at[0:7], c2r)
-    gathered = uu[...].reshape(128, 128)
+    arrived(uo.at[0:7], c2r)
+    gathered = uo[:, 0:16].reshape(128, 128)
     ups = []
     for i in range(2):
         up = jnp.where(up_lanes, dot(pu[i], gathered), 0.0)
         up = up + pltpu.roll(up, 64, 1)
         up = up + pltpu.roll(up, 32, 1)
         ups.append((up[:, 0:16].astype(BF), pltpu.roll(up, 112, 1)[:, 0:16].astype(BF)))
-    arrived(uo.at[0:7], d2r)
-    gathered = uo[...].reshape(256, 128)
+    gathered = uo[:, 16:48].reshape(256, 128)
     for h in range(8):
         dm[h * 128 : h * 128 + 128, :] = jnp.where(down_lanes, dot(pm[h], gathered), 0.0).astype(BF)
     arrived(zr, tr)
@@ -383,8 +390,7 @@
 
     left(r1.at[0:7], a1s)
     left(gt.at[:, 0:7168], a2s)
-    left(uu.at[0:7], c2s)
-    left(uo.at[0:7], d2s)
+    left(uo.at[0:7], c2s)
     left(zs, ts)
     left(zor.at[1:4], os)
     left(ps, pss)
@@ -436,14 +442,14 @@
             v((32, 4096), BF), v((2, 16, 8, 128), BF), v((32, 256, 128), BF), v((8192, 128), BF), v((1024, 4096), BF),
             v((32, 64), BF), v((2, 2, 32), BF), v((8, 2, 32), BF), v((32, 64), BF),
             v((64, 8192), BF), v((16, 16, 128), F32), v((8, 2, 16, 128), BF), v((8, 4, 16, 128), BF),
-            v((16, 8192), BF), v((8, 16, 128), BF), v((8, 32, 128), BF), v((64, 8192), BF), v((2, 128, 128), BF), v((8, 128, 256), BF), v((1024, 128), BF),
+            v((16, 8192), BF), v((8, 48, 128), BF), v((64, 8192), BF), v((2, 128, 128), BF), v((8, 128, 256), BF), v((1024, 128), BF),
             v((16, 32), F32), v((16, 32), F32),
             v((64, 16), BF), v((64, 16), BF), v((8, 128), F32), v((4, 8, 128), F32),
             v((16, 16, 128), F32), v((16, 16, 128), F32), v((16, 16, 128), F32), v((256, 128), F32),
             v((32, 1024), BF), v((128, 2048), BF),
             v((32, 2048), BF), v((32, 2048), BF), v((32, 2048), BF), v((32, 2048), BF), v((32, 2048), BF),
-            v((32, 128), F32), v((32, 128), F32), v((2, 2, 16, 128), BF), v((64, 128), F32), pltpu.SMEM((16,), jnp.int32),
-            dma((10,)), dma((22,)), dma((2048 // WIDTH,)), dma((2048 // WIDTH,)),
+            v((32, 128), F32), v((32, 128), F32), v((2, 2, 16, 128), BF), v((64, 128), F32), v((16, 16, 256), F32), v((16, 16, 256), BF), pltpu.SMEM((16,), jnp.int32),
+            dma((10,)), dma((20,)), dma((2048 // WIDTH,)), dma((2048 // WIDTH,)), dma((8,)),
         ],
         compiler_params=pltpu.CompilerParams(
             collective_id=0, has_side_effects=True, vmem_limit_bytes=40 * 1024 * 1024

time: 32 us -> 31.7 us (level)
  no operation moved by 1% of the time
where the time goes in v1:
time: 31.7 us; the launch traced here: 31.5 us
  Pallas kernels  30.9 us (97%)
  between operations  0.64 us (2%)
    pallas_call x1, Pallas kernels, local(): pl.pallas_call(kernel, out_shape=(pltpu.VMEM((32, 4096), BF), pltpu.VMEM(...  30.2 us
    pallas_call x1, Pallas kernels, local(): pl.pallas_call(store, out_shape=(pltpu.HBM((32, 4096), BF), pltpu.HBM((2,...  0.72 us

profile of v1, /device:TPU:1, one launch (start us, length us, event | category | flops | bytes accessed | tf_op | source)
XLA Modules:
  0.0 31.5 jit_solution(6010574659129436601)
XLA Ops:
  0.6 30.2 %shard_map.113 = (bf16[32,4096]{1,0:T(8,128)(2,1)S(1)}, bf16[2,2,16,128]{3,2,1,0:T(8,128)(2,1)S(1)}) custom-call(bf16[32,4096]{1,0:T(8,128)(2,1)} %bitcast.15, bf16[2,16,8,128]{3,2,1,0:T(8,128)(2,1)} %q_hbm.1, bf16[32,256,128]{2,1,0:T(8,128)(2,1)} %bitcast.13, s32[16]{0:T(128)} %len_hbm.1, bf16[8192,128]{1,0:T(8,128)(2,1)} %bitcast.14, ...), custom_call_target="tpu_custom_call" | custom-call | tf_op jit(solution)/shard_map/pallas_call | solution.py:436
  30.8 0.7 %shard_map.114 = (bf16[32,4096]{1,0:T(8,128)(2,1)}, bf16[2,2,16,128]{3,2,1,0:T(8,128)(2,1)}) custom-call(bf16[32,4096]{1,0:T(8,128)(2,1)S(1)} %get-tuple-element.6.att_in, bf16[2,2,16,128]{3,2,1,0:T(8,128)(2,1)S(1)} %get-tuple-element.7.nkv_in), custom_call_target="tpu_custom_call" | custom-call | tf_op jit(solution)/shard_map/pallas_call | solution.py:458

commit v2 on v1

--- a/solution.py
+++ b/solution.py
@@ -349,6 +349,8 @@
 
     lax.fori_loop(0, 2048 // WIDTH, give, 0)
 
+    keep(0, 0)
+
     for s in range(2):
         nst[s, 0] = key[s * 16 : s * 16 + 16]
         nst[s, 1] = value[s * 16 : s * 16 + 16]
@@ -367,7 +369,7 @@
     for k in (2, 3, 1):
         remote(zos, zor.at[k], os, orr, g, tensor_of(k)).start()
 
-    lax.fori_loop(0, 2048 // WIDTH, keep, 0)
+    lax.fori_loop(1, 2048 // WIDTH, keep, 0)
 
     @pl.when(yh == c)
     def _():

time: 31.7 us -> 31.5 us (level)
  no operation moved by 1% of the time
where the time goes in v2:
time: 31.5 us; the launch traced here: 31.4 us
  Pallas kernels  30.7 us (97%)
  between operations  0.64 us (2%)
    pallas_call x1, Pallas kernels, local(): pl.pallas_call(kernel, out_shape=(pltpu.VMEM((32, 4096), BF), pltpu.VMEM(...  30 us
    pallas_call x1, Pallas kernels, local(): pl.pallas_call(store, out_shape=(pltpu.HBM((32, 4096), BF), pltpu.HBM((2,...  0.72 us

profile of v2, /device:TPU:1, one launch (start us, length us, event | category | flops | bytes accessed | tf_op | source)
XLA Modules:
  0.0 31.4 jit_solution(11562214967538051473)
XLA Ops:
  0.6 30.0 %shard_map.113 = (bf16[32,4096]{1,0:T(8,128)(2,1)S(1)}, bf16[2,2,16,128]{3,2,1,0:T(8,128)(2,1)S(1)}) custom-call(bf16[32,4096]{1,0:T(8,128)(2,1)} %bitcast.15, bf16[2,16,8,128]{3,2,1,0:T(8,128)(2,1)} %q_hbm.1, bf16[32,256,128]{2,1,0:T(8,128)(2,1)} %bitcast.13, s32[16]{0:T(128)} %len_hbm.1, bf16[8192,128]{1,0:T(8,128)(2,1)} %bitcast.14, ...), custom_call_target="tpu_custom_call" | custom-call | tf_op jit(solution)/shard_map/pallas_call | solution.py:438
  30.7 0.7 %shard_map.114 = (bf16[32,4096]{1,0:T(8,128)(2,1)}, bf16[2,2,16,128]{3,2,1,0:T(8,128)(2,1)}) custom-call(bf16[32,4096]{1,0:T(8,128)(2,1)S(1)} %get-tuple-element.6.att_in, bf16[2,2,16,128]{3,2,1,0:T(8,128)(2,1)S(1)} %get-tuple-element.7.nkv_in), custom_call_target="tpu_custom_call" | custom-call | tf_op jit(solution)/shard_map/pallas_call | solution.py:460

commit v3 on v2

--- a/solution.py
+++ b/solution.py
@@ -220,6 +220,11 @@
         acc[r] = dot(pe[r], kv[16 + r])
     u[...] = jnp.zeros_like(u)
 
+    @pl.when(yh == c)
+    def _():
+        for k in (4, 3, 5, 2, 6, 1, 7):
+            remote(gb.at[z, x], gb.at[z, x], b1s, b1r, group_of(yh, lax.rem(z + k, 8), x), t).start()
+
     lane16 = lax.broadcasted_iota(jnp.int32, (16, 128), 1)
     block = yh * 4 + x
     arrived(r1.at[0:7], a1r)
@@ -240,11 +245,6 @@
     for k in (6, 2, 5, 7, 4, 1, 3):
         yh_, x_ = xy_peer(k)
         remote(uo.at[block], uo.at[block], c2s, c2r, group_of(yh_, z, x_), t).start()
-
-    @pl.when(yh == c)
-    def _():
-        for k in (4, 3, 5, 2, 6, 1, 7):
-            remote(gb.at[z, x], gb.at[z, x], b1s, b1r, group_of(yh, lax.rem(z + k, 8), x), t).start()
 
 
     def down_part(from_block):

time: 31.5 us -> 31.5 us (level)
  no operation moved by 1% of the time
where the time goes in v3:
time: 31.5 us; the launch traced here: 31.4 us
  Pallas kernels  30.7 us (97%)
  between operations  0.64 us (2%)
    pallas_call x1, Pallas kernels, local(): pl.pallas_call(kernel, out_shape=(pltpu.VMEM((32, 4096), BF), pltpu.VMEM(...  30 us
    pallas_call x1, Pallas kernels, local(): pl.pallas_call(store, out_shape=(pltpu.HBM((32, 4096), BF), pltpu.HBM((2,...  0.72 us

profile of v3, /device:TPU:1, one launch (start us, length us, event | category | flops | bytes accessed | tf_op | source)
XLA Modules:
  0.0 31.4 jit_solution(10539641712184308731)
XLA Ops:
  0.6 30.0 %shard_map.113 = (bf16[32,4096]{1,0:T(8,128)(2,1)S(1)}, bf16[2,2,16,128]{3,2,1,0:T(8,128)(2,1)S(1)}) custom-call(bf16[32,4096]{1,0:T(8,128)(2,1)} %bitcast.15, bf16[2,16,8,128]{3,2,1,0:T(8,128)(2,1)} %q_hbm.1, bf16[32,256,128]{2,1,0:T(8,128)(2,1)} %bitcast.13, s32[16]{0:T(128)} %len_hbm.1, bf16[8192,128]{1,0:T(8,128)(2,1)} %bitcast.14, ...), custom_call_target="tpu_custom_call" | custom-call | tf_op jit(solution)/shard_map/pallas_call | solution.py:438
  30.7 0.7 %shard_map.114 = (bf16[32,4096]{1,0:T(8,128)(2,1)}, bf16[2,2,16,128]{3,2,1,0:T(8,128)(2,1)}) custom-call(bf16[32,4096]{1,0:T(8,128)(2,1)S(1)} %get-tuple-element.6.att_in, bf16[2,2,16,128]{3,2,1,0:T(8,128)(2,1)S(1)} %get-tuple-element.7.nkv_in), custom_call_target="tpu_custom_call" | custom-call | tf_op jit(solution)/shard_map/pallas_call | solution.py:460
